TPU v7x, 512 devices: a whole 4x4x16 slice. The times are simulated.
512 devices in a mesh: seq: 64 (over z, y), segment: 8 (over x, core).
Axes of the slice: x: 4, y: 4, z: 16, core: 2. Of those that a mesh axis runs over, the one named last changes fastest.
Arguments:
- queries: bfloat16 [8, 23552, 1024], P('segment', 'seq'), may hold values from -6 to 6
- key_rows: bfloat16 [8, 23552, 1024], P('segment', 'seq'), may hold values from -6 to 6
- value_rows: bfloat16 [8, 23552, 1024], P('segment', 'seq'), may hold values from -6 to 6
- out_weight: bfloat16 [8, 1024, 1024], P('segment'), may hold values from -0.1875 to 0.1875
Outputs:
- handed: bfloat16 [8, 23552, 1024], P('segment', 'seq')
All inputs are finite; a program needn't handle non-finite values.
Results may differ from a plain program's by a relative error of at most 0.0058.
Values may be sent and summed in bfloat16 or wider, within the bound.
No kernel may reach another device: no remote copies, remote signals or barrier semaphores. Data moves between devices by JAX's collectives and lax.ppermute only.
A program may use at most 128 MiB of HBM per device.

v0:
```python
import jax
import jax.numpy as jnp
from jax import lax
from jax.sharding import PartitionSpec as P

HEADS = 8
HEAD_DIM = 128


epsilon = 1e-06


def prefix(part, axis, combine, identity):
    place = lax.axis_index(axis)
    gathered = lax.all_gather(part, axis)
    state = jnp.zeros_like(part) + jnp.asarray(identity, part.dtype)

    def one(step, state):
        return combine(state, lax.dynamic_index_in_dim(gathered, step, 0, False))

    return lax.fori_loop(0, place, one, state)


def shifted(block, axis, distance):
    devices = range(lax.axis_size(axis))
    route = [((i - distance) % len(devices), i) for i in devices]
    return lax.ppermute(block, axis, route)


def heads_of(block):
    return block.reshape(block.shape[0], HEADS, HEAD_DIM)


def add_states(earlier, later):
    return earlier + later


def shards(queries, key_rows, value_rows, out_weight):
    query_heads = heads_of(queries[0])
    key_heads = heads_of(key_rows[0])
    value_heads = heads_of(value_rows[0])
    total_rows = query_heads.shape[0]
    states = jnp.einsum("thd,the->hde", key_heads, value_heads, preferred_element_type=jnp.float32)
    prior = prefix(states, "seq", add_states, jnp.zeros_like(states))
    carried = prior.astype(jnp.bfloat16)
    weight = out_weight[0]
    scores = jnp.einsum("ihd,jhd->hij", query_heads, key_heads, preferred_element_type=jnp.float32)
    row_ids = lax.broadcasted_iota(jnp.int32, (total_rows, total_rows), 0)
    col_ids = lax.broadcasted_iota(jnp.int32, (total_rows, total_rows), 1)
    causal = col_ids <= row_ids
    local_part = jnp.where(causal[None], scores, jnp.zeros_like(scores)).astype(jnp.bfloat16)
    mixed_heads = jnp.einsum(
        "hij,jhe->ihe", local_part, value_heads, preferred_element_type=jnp.float32
    )
    mixed_heads = mixed_heads + jnp.einsum(
        "ihd,hde->ihe", query_heads, carried, preferred_element_type=jnp.float32
    )
    normed = mixed_heads * lax.rsqrt(
        jnp.mean(mixed_heads * mixed_heads, axis=2, keepdims=True) + epsilon
    )
    normed = normed.reshape(total_rows, HEADS * HEAD_DIM).astype(jnp.bfloat16)
    branch = jnp.dot(normed, weight, preferred_element_type=jnp.float32).astype(jnp.bfloat16)
    handed = shifted(branch, "segment", 1)
    return handed[None]


def solution(mesh):
    return jax.shard_map(
        shards,
        mesh=mesh,
        in_specs=(
            P("segment", "seq", None),
            P("segment", "seq", None),
            P("segment", "seq", None),
            P("segment", None, None),
        ),
        out_specs=P("segment", "seq", None),
        check_vma=False,
    )
```

profile of v0, /device:TPU:504, one launch (start us, length us, event | category | flops | bytes accessed | tf_op | source)
XLA Modules:
  0.0 397.3 jit_solution(9617602889158188901)
XLA Ops:
  6.5 1.4 copy.24
  9.1 1.3 fusion.13
  10.4 1.3 copy.22
  11.7 4.2 %fusion = f32[8,368,128]{2,1,0:T(8,128)} fusion(pred[368,368]{1,0:T(8,128)(4,1)S(1)} %iota_compare_fusion, bf16[368,8,128]{2,1,0:T(8,128)(2,1)} %bitcast.34, bf16[368,8,128]{2,1,0:T(8,128)(2,1)} %bitcast.36, bf16[368,8,128]{2,1,0:T(8,128)(2,1)S(1)} %bitcast.31), kind=kOutput, calls=%fused_computation.2 | convolution fusion | flops 556863488 | bytes 3903744 | tf_op jit(solution)/shard_map/hij,jhe->ihe/dot_general | solution.py:52
  15.9 283.2 %all-gather.3.cloned.1.call-done = f32[512,128,128]{2,1,0:T(8,128)} async-done(((f32[8,128,128]{2,1,0:T(8,128)}), f32[512,128,128]{2,1,0:T(8,128)}) %all-gather.3.cloned.1.call-update) | async-done | bytes 33554448 | tf_op jit(solution)/shard_map/all_gather | solution.py:15
  299.2 75.0 %while.10 = (s32[]{:T(128)}, f32[8,128,128]{2,1,0:T(8,128)S(1)}, s32[]{:T(128)}, f32[64,8,128,128]{3,2,1,0:T(8,128)}, s32[]{:T(128)}, /*index=5*/s32[]{:T(128)}, s32[]{:T(128)}) while((s32[]{:T(128)}, f32[8,128,128]{2,1,0:T(8,128)S(1)}, s32[]{:T(128)}, f32[64,8,128,128]{3,2,1,0:T(8,128)}, s32[]{:T(128)}, /*index=5*/s32[]{:T(128)}, ...), condition=%wide.region_1.2_spmd, body=%wide.region_0.1_spmd.sunk | while | flops 131077 | bytes 1572987 | solution.py:21
  299.2 1.2 bitcast_add_fusion.3
  300.4 1.2 bitcast_add_fusion.3
  301.6 1.2 bitcast_add_fusion.3
  302.8 1.2 bitcast_add_fusion.3
  304.0 1.2 bitcast_add_fusion.3
  305.2 1.2 bitcast_add_fusion.3
  306.3 1.2 bitcast_add_fusion.3
  307.5 1.2 bitcast_add_fusion.3
  308.7 1.2 bitcast_add_fusion.3
  309.9 1.2 bitcast_add_fusion.3
  311.1 1.2 bitcast_add_fusion.3
  312.3 1.2 bitcast_add_fusion.3
  313.5 1.2 bitcast_add_fusion.3
  314.7 1.2 bitcast_add_fusion.3
  315.9 1.2 bitcast_add_fusion.3
  317.1 1.2 bitcast_add_fusion.3
  318.3 1.2 bitcast_add_fusion.3
  319.4 1.2 bitcast_add_fusion.3
  320.6 1.2 bitcast_add_fusion.3
  321.8 1.2 bitcast_add_fusion.3
  323.0 1.2 bitcast_add_fusion.3
  324.2 1.2 bitcast_add_fusion.3
  325.4 1.2 bitcast_add_fusion.3
  326.6 1.2 bitcast_add_fusion.3
  327.8 1.2 bitcast_add_fusion.3
  329.0 1.2 bitcast_add_fusion.3
  330.2 1.2 bitcast_add_fusion.3
  333.7 1.2 bitcast_add_fusion.3
  337.3 1.2 bitcast_add_fusion.3
  340.9 1.2 bitcast_add_fusion.3
  343.3 1.2 bitcast_add_fusion.3
  346.8 1.2 bitcast_add_fusion.3
  350.4 1.2 bitcast_add_fusion.3
  352.8 1.2 bitcast_add_fusion.3
  356.4 1.2 bitcast_add_fusion.3
  359.9 1.2 bitcast_add_fusion.3
  363.5 1.2 bitcast_add_fusion.3
  365.9 1.2 bitcast_add_fusion.3
  369.5 1.2 bitcast_add_fusion.3
  373.0 1.2 bitcast_add_fusion.3
  374.2 2.1 multiply_reduce_fusion
  377.4 12.3 %collective-permute-done = bf16[368,1024]{1,0:T(8,128)(2,1)S(1)} collective-permute-done((bf16[368,1024]{1,0:T(8,128)(2,1)S(1)}, bf16[368,1024]{1,0:T(8,128)(2,1)S(1)}, u32[]{:S(2)}, u32[]{:S(2)}) %collective-permute-start) | collective-permute-done | bytes 753696 | tf_op jit(solution)/shard_map/ppermute | solution.py:27
  (40 shorter events, 30.0 us)
Async XLA Ops:
  6.5 369.8 %copy-start = (bf16[1,1024,1024]{2,1,0:T(8,128)(2,1)S(1)}, bf16[1,1024,1024]{2,1,0:T(8,128)(2,1)}, u32[]{:S(2)}) copy-start(bf16[1,1024,1024]{2,1,0:T(8,128)(2,1)} %param.9) | copy-start | bytes 6291460
  6.5 1.5 copy-start.3
  6.5 292.6 %all-gather.3.cloned.1.call-start = ((), (), s32[]{:S(2)}) async-start(), calls=%async_computation | async-start | bytes 34078720 | tf_op jit(solution)/shard_map/all_gather | solution.py:15
  8.0 0.9 copy-start.1
  8.2 0.9 copy-start.2
  377.3 12.3 %collective-permute-start = (bf16[368,1024]{1,0:T(8,128)(2,1)S(1)}, bf16[368,1024]{1,0:T(8,128)(2,1)S(1)}, u32[]{:S(2)}, u32[]{:S(2)}) collective-permute-start(bf16[368,1024]{1,0:T(8,128)(2,1)S(1)} %fusion.7), channel_id=1, source_target_pairs={{7,0},{0,1},{1,2},{2,3},{3,4},{4,5},{5,6},{6,7},{15,8},{8,9},{9,10... | collective-permute-start | bytes 2261000 | tf_op jit(solution)/shard_map/ppermute | solution.py:27
Sparse Core Ops, SparseCore 0:
  10.5 288.5 all-gather.2
where the time goes:
time: 401 us; the launch traced here: 397 us
  waiting for transfers between devices  295 us (74%)
  other arithmetic  73.7 us (18%)
  between operations  13.5 us (3%)
  matrix products  8.56 us (2%)
  local copies, waits for them, and re-layouts  4.7 us (1%)
    all_gather x1, waiting for transfers between devices, prefix(): gathered = lax.all_gather(part, axis)  283 us
    add x63, other arithmetic, add_states(): return earlier + later  73.6 us
    ppermute x1, waiting for transfers between devices, shifted(): return lax.ppermute(block, axis, route)  12.3 us
  transfers between devices with their start and end apart: 2, of which 2 were waited for; matrix products, arithmetic and copies ran while one was open for 1% of the time, Pallas kernels for 0%

commit v1 on v0

v1 whole, which is shorter than its diff:
```python
import jax
import jax.numpy as jnp
from jax import lax
from jax.experimental import pallas as pl
from jax.experimental.pallas import tpu as pltpu
from jax.sharding import PartitionSpec as P

HEADS = 8
HEAD_DIM = 128
GROUP = 16
EPSILON = 1e-06

F32 = jnp.float32
BF16 = jnp.bfloat16
VMEM = pl.BlockSpec(memory_space=pltpu.VMEM)
SMEM = pl.BlockSpec(memory_space=pltpu.SMEM)


def call(body, out_shape, args, specs, flops, nbytes, limit=24 << 20, scratch=()):
    return pl.pallas_call(
        body,
        out_shape=out_shape,
        in_specs=specs,
        out_specs=jax.tree.map(lambda _: VMEM, out_shape),
        scratch_shapes=scratch,
        compiler_params=pltpu.CompilerParams(vmem_limit_bytes=limit),
        cost_estimate=pl.CostEstimate(flops=flops, bytes_accessed=nbytes, transcendentals=0),
    )(*args)


def head(h):
    return slice(h * HEAD_DIM, (h + 1) * HEAD_DIM)


def states_kernel(k_ref, v_ref, out_ref):
    for h in range(HEADS):
        state = lax.dot_general(
            k_ref[:, head(h)], v_ref[:, head(h)], (((0,), (0,)), ((), ())), preferred_element_type=F32
        )
        out_ref[head(h), :] = state.astype(BF16)


def local_kernel(q_ref, k_ref, v_ref, out_ref):
    rows = q_ref.shape[0]
    row_ids = lax.broadcasted_iota(jnp.int32, (rows, rows), 0)
    col_ids = lax.broadcasted_iota(jnp.int32, (rows, rows), 1)
    causal = col_ids <= row_ids
    for h in range(HEADS):
        scores = lax.dot_general(
            q_ref[:, head(h)], k_ref[:, head(h)], (((1,), (1,)), ((), ())), preferred_element_type=F32
        )
        scores = jnp.where(causal, scores, 0.0).astype(BF16)
        out_ref[:, head(h)] = jnp.dot(scores, v_ref[:, head(h)], preferred_element_type=F32)


def total_kernel(slices_ref, out_ref):
    acc = slices_ref[0].astype(F32)
    for m in range(1, slices_ref.shape[0]):
        acc = acc + slices_ref[m].astype(F32)
    out_ref[...] = acc


def prefix_kernel(group_ref, slices_ref, totals_ref, out_ref):
    group = group_ref[0]
    acc = jnp.zeros(out_ref.shape[1:], F32)
    for g in range(totals_ref.shape[0] - 1):
        acc = acc + jnp.where(g < group, totals_ref[g], 0.0)
    for m in range(slices_ref.shape[0]):
        out_ref[m] = acc.astype(BF16)
        acc = acc + slices_ref[m].astype(F32)


def branch_kernel(q_ref, local_ref, carried_ref, w_ref, out_ref, normed_ref):
    for h in range(HEADS):
        mixed = local_ref[:, head(h)] + jnp.dot(
            q_ref[:, head(h)], carried_ref[head(h), :], preferred_element_type=F32
        )
        scale = lax.rsqrt(jnp.mean(mixed * mixed, axis=1, keepdims=True) + EPSILON)
        normed_ref[:, head(h)] = (mixed * scale).astype(BF16)
    out_ref[...] = jnp.dot(normed_ref[...], w_ref[...], preferred_element_type=F32).astype(BF16)


def shards(queries, key_rows, value_rows, out_weight):
    q, k, v, w = queries[0], key_rows[0], value_rows[0], out_weight[0]
    rows, width = q.shape
    blocks = lax.axis_size("seq")
    near = [[g * GROUP + m for m in range(GROUP)] for g in range(blocks // GROUP)]
    far = [[g * GROUP + m for g in range(blocks // GROUP)] for m in range(GROUP)]
    piece = (HEADS * HEAD_DIM // GROUP, HEAD_DIM)

    states = call(
        states_kernel, jax.ShapeDtypeStruct((HEADS * HEAD_DIM, HEAD_DIM), BF16), (k, v), [VMEM] * 2,
        2 * rows * width * HEAD_DIM, 2 * rows * width * 2,
    )
    slices = lax.all_to_all(states.reshape(GROUP, *piece), "seq", 0, 0, axis_index_groups=near)
    total = call(
        total_kernel, jax.ShapeDtypeStruct(piece, F32), (slices,), [VMEM], 1 << 17, 1 << 19,
    )
    totals = lax.all_gather(total, "seq", axis_index_groups=far)
    local = call(
        local_kernel, jax.ShapeDtypeStruct((rows, width), F32), (q, k, v), [VMEM] * 3,
        4 * rows * rows * width, 5 * rows * width * 2,
    )
    group = (lax.axis_index("seq") // GROUP).astype(jnp.int32).reshape(1)
    prefixes = call(
        prefix_kernel, jax.ShapeDtypeStruct((GROUP, *piece), BF16), (group, slices, totals),
        [SMEM, VMEM, VMEM], 1 << 18, 1 << 20,
    )
    carried = lax.all_to_all(prefixes, "seq", 0, 0, axis_index_groups=near).reshape(-1, HEAD_DIM)
    branch = call(
        branch_kernel, jax.ShapeDtypeStruct((rows, width), BF16), (q, local, carried, w), [VMEM] * 4,
        2 * rows * width * (width + HEAD_DIM), 6 << 20, scratch=[pltpu.VMEM((rows, width), BF16)],
    )
    size = lax.axis_size("segment")
    handed = lax.ppermute(branch, "segment", [((i - 1) % size, i) for i in range(size)])
    return handed[None]


def solution(mesh):
    return jax.shard_map(
        shards,
        mesh=mesh,
        in_specs=(
            P("segment", "seq", None),
            P("segment", "seq", None),
            P("segment", "seq", None),
            P("segment", None, None),
        ),
        out_specs=P("segment", "seq", None),
        check_vma=False,
    )
```

time: 401 us -> 77.2 us (0.19)
  the two profiles are of different devices: /device:TPU:504 before, /device:TPU:6 now
where the time goes in v1:
time: 77.2 us; the launch traced here: 76.6 us
  waiting for transfers between devices  28.7 us (37%)
  blocking collectives  23.5 us (30%)
  starting transfers between devices  12.2 us (16%)
  local copies, waits for them, and re-layouts  6.95 us (9%)
  Pallas kernels  5.1 us (7%)
    all_gather x1, blocking collectives, shards(): totals = lax.all_gather(total, 'seq', axis_index_groups=far)  23.5 us
    ppermute x1, waiting for transfers between devices, shards(): lax.ppermute(branch, 'segment', [((i - 1) % size, i) for i in range(size)])  11.1 us
    all_to_all x1, waiting for transfers between devices, shards(): lax.all_to_all(states.reshape(GROUP, *piece), 'seq', 0, 0, axis_index_gro...  10.7 us
    all_to_all x1, starting transfers between devices, shards(): lax.all_to_all(states.reshape(GROUP, *piece), 'seq', 0, 0, axis_index_gro...  8.64 us
    all_to_all x1, waiting for transfers between devices, shards(): lax.all_to_all(prefixes, 'seq', 0, 0, axis_index_groups=near)  7 us
    unnamed x15, local copies, waits for them, and re-layouts  6.95 us
    pallas_call x5, Pallas kernels, call(): pl.pallas_call(body, out_shape=out_shape, in_specs=specs, out_specs=jax.t...  5.1 us
    all_to_all x1, starting transfers between devices, shards(): lax.all_to_all(prefixes, 'seq', 0, 0, axis_index_groups=near)  3.59 us
  transfers between devices with their start and end apart: 3, of which 3 were waited for; matrix products, arithmetic and copies ran while one was open for 0% of the time, Pallas kernels for 2%

profile of v1, /device:TPU:6, one launch (start us, length us, event | category | flops | bytes accessed | tf_op | source)
XLA Modules:
  0.0 76.6 jit_solution(366944881965433912)
XLA Ops:
  0.0 0.0 copy-start
  0.0 1.1 %copy-done = bf16[1,368,1024]{2,1,0:T(8,128)(2,1)S(1)} copy-done((bf16[1,368,1024]{2,1,0:T(8,128)(2,1)S(1)}, bf16[1,368,1024]{2,1,0:T(8,128)(2,1)}, u32[]{:S(2)}) %copy-start) | copy-done | bytes 753688
  1.1 0.0 copy-start.2
  1.1 1.1 %copy-done.2 = bf16[1,368,1024]{2,1,0:T(8,128)(2,1)S(1)} copy-done((bf16[1,368,1024]{2,1,0:T(8,128)(2,1)S(1)}, bf16[1,368,1024]{2,1,0:T(8,128)(2,1)}, u32[]{:S(2)}) %copy-start.2) | copy-done | bytes 753688
  2.2 0.0 copy-start.1
  2.2 0.0 copy-start.3
  2.2 1.1 %shard_map.47 = bf16[1024,128]{1,0:T(8,128)(2,1)} custom-call(bf16[368,1024]{1,0:T(8,128)(2,1)S(1)} %bitcast.9, bf16[368,1024]{1,0:T(8,128)(2,1)S(1)} %bitcast.11), custom_call_target="tpu_custom_call" | custom-call | flops 96468992 | bytes 1507328 | tf_op jit(solution)/shard_map/pallas_call | solution.py:20
  3.4 8.6 %all-to-all-start = ((bf16[16,64,128]{2,1,0:T(8,128)(2,1)}), bf16[16,64,128]{2,1,0:T(8,128)(2,1)S(1)}, u32[]{:S(2)}, u32[]{:S(2)}) async-start(bf16[16,64,128]{2,1,0:T(8,128)(2,1)} %bitcast.4), calls=%async_computation | async-start | bytes 524288 | tf_op jit(solution)/shard_map/all_to_all | solution.py:95
  12.0 10.7 %all-to-all-done.slices_ref = bf16[16,64,128]{2,1,0:T(8,128)(2,1)S(1)} async-done(((bf16[16,64,128]{2,1,0:T(8,128)(2,1)}), bf16[16,64,128]{2,1,0:T(8,128)(2,1)S(1)}, u32[]{:S(2)}, u32[]{:S(2)}) %all-to-all-start) | async-done | bytes 262176 | tf_op jit(solution)/shard_map/all_to_all | solution.py:95
  22.7 23.5 %all-gather = f32[256,128]{1,0:T(8,128)S(1)} all-gather(f32[64,128]{1,0:T(8,128)S(1)} %shard_map.48), channel_id=2, replica_groups={{0,128,256,384},{8,136,264,392},{16,144,272,400},{24,152,280,408},{32,1..., dimensions={0}, use_global_device_ids=true | all-gather | bytes 163840 | tf_op jit(solution)/shard_map/all_gather | solution.py:99
  46.2 0.8 shard_map.49
  47.0 3.6 %all-to-all-start.1 = ((bf16[16,64,128]{2,1,0:T(8,128)(2,1)}), bf16[16,64,128]{2,1,0:T(8,128)(2,1)S(1)}, u32[]{:S(2)}, u32[]{:S(2)}) async-start(bf16[16,64,128]{2,1,0:T(8,128)(2,1)} %shard_map.49), calls=%async_computation.1 | async-start | bytes 524288 | tf_op jit(solution)/shard_map/all_to_all | solution.py:109
  50.6 0.0 copy-done.1
  50.6 0.0 copy-done.3
  50.6 0.0 copy-start.4
  50.6 1.1 %copy-done.4 = bf16[1,368,1024]{2,1,0:T(8,128)(2,1)S(1)} copy-done((bf16[1,368,1024]{2,1,0:T(8,128)(2,1)S(1)}, bf16[1,368,1024]{2,1,0:T(8,128)(2,1)}, u32[]{:S(2)}) %copy-start.4) | copy-done | bytes 753688
  51.7 1.8 %shard_map.46.local_ref = f32[368,1024]{1,0:T(8,128)S(1)} custom-call(bf16[368,1024]{1,0:T(8,128)(2,1)S(1)} %bitcast.13, bf16[368,1024]{1,0:T(8,128)(2,1)S(1)} %bitcast.10, bf16[368,1024]{1,0:T(8,128)(2,1)S(1)} %bitcast.12), custom_call_target="tpu_custom_call" | custom-call | flops 554696704 | bytes 3768320 | tf_op jit(solution)/shard_map/pallas_call | solution.py:20
  53.6 7.0 %all-to-all-done.1 = bf16[16,64,128]{2,1,0:T(8,128)(2,1)S(1)} async-done(((bf16[16,64,128]{2,1,0:T(8,128)(2,1)}), bf16[16,64,128]{2,1,0:T(8,128)(2,1)S(1)}, u32[]{:S(2)}, u32[]{:S(2)}) %all-to-all-start.1) | async-done | bytes 262176 | tf_op jit(solution)/shard_map/all_to_all | solution.py:109
  60.6 0.0 copy-start.5
  60.6 1.1 %copy-done.5 = bf16[1,368,1024]{2,1,0:T(8,128)(2,1)S(1)} copy-done((bf16[1,368,1024]{2,1,0:T(8,128)(2,1)S(1)}, bf16[1,368,1024]{2,1,0:T(8,128)(2,1)}, u32[]{:S(2)}) %copy-start.5) | copy-done | bytes 753688
  61.7 0.0 copy-start.6
  61.7 1.6 %copy-done.6 = bf16[1,1024,1024]{2,1,0:T(8,128)(2,1)S(1)} copy-done((bf16[1,1024,1024]{2,1,0:T(8,128)(2,1)S(1)}, bf16[1,1024,1024]{2,1,0:T(8,128)(2,1)}, u32[]{:S(2)}) %copy-start.6) | copy-done | bytes 2097176
  63.3 1.3 %shard_map.50 = bf16[368,1024]{1,0:T(8,128)(2,1)S(1)} custom-call(bf16[368,1024]{1,0:T(8,128)(2,1)S(1)} %bitcast.14, f32[368,1024]{1,0:T(8,128)S(1)} %shard_map.46.local_ref, bf16[1024,128]{1,0:T(8,128)(2,1)S(1)} %bitcast.16, bf16[1024,1024]{1,0:T(8,128)(2,1)S(1)} %bitcast.15), custom_call_target="tpu_custom_call" | custom-call | flops 868220928 | bytes 6291456 | tf_op jit(solution)/shard_map/pallas_call | solution.py:20
  64.6 0.0 collective-permute-start
  64.6 11.1 %collective-permute-done = bf16[368,1024]{1,0:T(8,128)(2,1)S(1)} collective-permute-done((bf16[368,1024]{1,0:T(8,128)(2,1)S(1)}, bf16[368,1024]{1,0:T(8,128)(2,1)S(1)}, u32[]{:S(2)}, u32[]{:S(2)}) %collective-permute-start) | collective-permute-done | bytes 753696 | tf_op jit(solution)/shard_map/ppermute | solution.py:115
  75.7 0.9 %copy.6 = bf16[1,368,1024]{2,1,0:T(8,128)(2,1)} copy(bf16[1,368,1024]{2,1,0:T(8,128)(2,1)S(1)} %bitcast.18) | data formatting | bytes 1507328
  (1 shorter events, 0.0 us)
Async XLA Ops:
  0.0 1.1 %copy-start = (bf16[1,368,1024]{2,1,0:T(8,128)(2,1)S(1)}, bf16[1,368,1024]{2,1,0:T(8,128)(2,1)}, u32[]{:S(2)}) copy-start(bf16[1,368,1024]{2,1,0:T(8,128)(2,1)} %param.5) | copy-start | bytes 2260996
  1.1 1.1 %copy-start.2 = (bf16[1,368,1024]{2,1,0:T(8,128)(2,1)S(1)}, bf16[1,368,1024]{2,1,0:T(8,128)(2,1)}, u32[]{:S(2)}) copy-start(bf16[1,368,1024]{2,1,0:T(8,128)(2,1)} %param.6) | copy-start | bytes 2260996
  2.2 48.3 %copy-start.1 = (bf16[1,368,1024]{2,1,0:T(8,128)(2,1)S(1)}, bf16[1,368,1024]{2,1,0:T(8,128)(2,1)}, u32[]{:S(2)}) copy-start(bf16[1,368,1024]{2,1,0:T(8,128)(2,1)} %param.5) | copy-start | bytes 2260996
  2.2 48.3 %copy-start.3 = (bf16[1,368,1024]{2,1,0:T(8,128)(2,1)S(1)}, bf16[1,368,1024]{2,1,0:T(8,128)(2,1)}, u32[]{:S(2)}) copy-start(bf16[1,368,1024]{2,1,0:T(8,128)(2,1)} %param.6) | copy-start | bytes 2260996
  3.4 19.3 %all-to-all-start = ((bf16[16,64,128]{2,1,0:T(8,128)(2,1)}), bf16[16,64,128]{2,1,0:T(8,128)(2,1)S(1)}, u32[]{:S(2)}, u32[]{:S(2)}) async-start(bf16[16,64,128]{2,1,0:T(8,128)(2,1)} %bitcast.4), calls=%async_computation | async-start | bytes 524288 | tf_op jit(solution)/shard_map/all_to_all | solution.py:95
  47.0 13.6 %all-to-all-start.1 = ((bf16[16,64,128]{2,1,0:T(8,128)(2,1)}), bf16[16,64,128]{2,1,0:T(8,128)(2,1)S(1)}, u32[]{:S(2)}, u32[]{:S(2)}) async-start(bf16[16,64,128]{2,1,0:T(8,128)(2,1)} %shard_map.49), calls=%async_computation.1 | async-start | bytes 524288 | tf_op jit(solution)/shard_map/all_to_all | solution.py:109
  50.6 1.1 %copy-start.4 = (bf16[1,368,1024]{2,1,0:T(8,128)(2,1)S(1)}, bf16[1,368,1024]{2,1,0:T(8,128)(2,1)}, u32[]{:S(2)}) copy-start(bf16[1,368,1024]{2,1,0:T(8,128)(2,1)} %param.4) | copy-start | bytes 2260996
  60.6 1.1 %copy-start.5 = (bf16[1,368,1024]{2,1,0:T(8,128)(2,1)S(1)}, bf16[1,368,1024]{2,1,0:T(8,128)(2,1)}, u32[]{:S(2)}) copy-start(bf16[1,368,1024]{2,1,0:T(8,128)(2,1)} %param.4) | copy-start | bytes 2260996
  61.7 1.6 %copy-start.6 = (bf16[1,1024,1024]{2,1,0:T(8,128)(2,1)S(1)}, bf16[1,1024,1024]{2,1,0:T(8,128)(2,1)}, u32[]{:S(2)}) copy-start(bf16[1,1024,1024]{2,1,0:T(8,128)(2,1)} %param.7) | copy-start | bytes 6291460
  64.6 11.1 %collective-permute-start = (bf16[368,1024]{1,0:T(8,128)(2,1)S(1)}, bf16[368,1024]{1,0:T(8,128)(2,1)S(1)}, u32[]{:S(2)}, u32[]{:S(2)}) collective-permute-start(bf16[368,1024]{1,0:T(8,128)(2,1)S(1)} %shard_map.50), channel_id=1, source_target_pairs={{7,0},{0,1},{1,2},{2,3},{3,4},{4,5},{5,6},{6,7},{15,8},{8,9},{9,10... | collective-permute-start | bytes 2261000 | tf_op jit(solution)/shard_map/ppermute | solution.py:115

commit v2 on v1

v2 whole, which is shorter than its diff:
```python
import jax
import jax.numpy as jnp
from jax import lax
from jax.experimental import pallas as pl
from jax.experimental.pallas import tpu as pltpu
from jax.sharding import PartitionSpec as P

HEADS = 8
HEAD_DIM = 128
GROUP = 16
SLAB = 2
EPSILON = 1e-06

F32 = jnp.float32
BF16 = jnp.bfloat16
VMEM = pl.BlockSpec(memory_space=pltpu.VMEM)
SMEM = pl.BlockSpec(memory_space=pltpu.SMEM)
ANY = pl.BlockSpec(memory_space=pl.ANY)


def call(body, out_shape, args, specs, flops, nbytes, out_specs=VMEM, limit=24 << 20, scratch=()):
    return pl.pallas_call(
        body,
        out_shape=out_shape,
        in_specs=specs,
        out_specs=out_specs,
        scratch_shapes=scratch,
        compiler_params=pltpu.CompilerParams(vmem_limit_bytes=limit),
        cost_estimate=pl.CostEstimate(flops=flops, bytes_accessed=nbytes, transcendentals=0),
    )(*args)


def head(h):
    return slice(h * HEAD_DIM, (h + 1) * HEAD_DIM)


def slab_copies(sources, targets, sem):
    width = SLAB * HEAD_DIM
    return [
        [
            pltpu.make_async_copy(
                source.at[:, pl.ds(s * width, width)],
                target.at[:, pl.ds(s * width, width)],
                sem.at[s, a],
            )
            for a, (source, target) in enumerate(zip(sources, targets))
        ]
        for s in range(HEADS // SLAB)
    ]


def states_kernel(k_hbm, v_hbm, out_ref, k_ref, v_ref, sem):
    copies = slab_copies((k_hbm, v_hbm), (k_ref, v_ref), sem)
    for slab in copies:
        for copy in slab:
            copy.start()
    for h in range(HEADS):
        if h % SLAB == 0:
            for copy in copies[h // SLAB]:
                copy.wait()
        state = lax.dot_general(
            k_ref[:, head(h)], v_ref[:, head(h)], (((0,), (0,)), ((), ())), preferred_element_type=F32
        )
        out_ref[head(h), :] = state.astype(BF16)


def local_kernel(q_hbm, k_hbm, v_hbm, after_ref, out_ref, k_ref, v_ref, sem):
    del after_ref
    rows = q_hbm.shape[0]
    q_ref, local_ref = out_ref.at[pl.ds(0, rows)], out_ref.at[pl.ds(rows, rows)]
    copies = slab_copies((q_hbm, k_hbm, v_hbm), (q_ref, k_ref, v_ref), sem)
    for slab in copies:
        for copy in slab:
            copy.start()
    row_ids = lax.broadcasted_iota(jnp.int32, (rows, rows), 0)
    col_ids = lax.broadcasted_iota(jnp.int32, (rows, rows), 1)
    causal = col_ids <= row_ids
    for h in range(HEADS):
        if h % SLAB == 0:
            for copy in copies[h // SLAB]:
                copy.wait()
        scores = lax.dot_general(
            q_ref[:, head(h)], k_ref[:, head(h)], (((1,), (1,)), ((), ())), preferred_element_type=F32
        )
        scores = jnp.where(causal, scores, 0.0).astype(BF16)
        local_ref[:, head(h)] = jnp.dot(
            scores, v_ref[:, head(h)], preferred_element_type=F32
        ).astype(BF16)


def total_kernel(slices_ref, out_ref):
    acc = slices_ref[0].astype(F32)
    for m in range(1, slices_ref.shape[0]):
        acc = acc + slices_ref[m].astype(F32)
    out_ref[...] = acc


def prefix_kernel(group_ref, slices_ref, totals_ref, out_ref):
    group = group_ref[0]
    acc = jnp.zeros(out_ref.shape[1:], F32)
    for g in range(totals_ref.shape[0] - 1):
        acc = acc + jnp.where(g < group, totals_ref[g], 0.0)
    for m in range(slices_ref.shape[0]):
        out_ref[m] = acc.astype(BF16)
        acc = acc + slices_ref[m].astype(F32)


def branch_kernel(pair_ref, carried_ref, w_ref, out_ref, normed_ref):
    rows = out_ref.shape[0]
    for h in range(HEADS):
        mixed = pair_ref[rows : 2 * rows, head(h)].astype(F32) + jnp.dot(
            pair_ref[0:rows, head(h)], carried_ref[head(h), :], preferred_element_type=F32
        )
        scale = lax.rsqrt(jnp.mean(mixed * mixed, axis=1, keepdims=True) + EPSILON)
        normed_ref[:, head(h)] = (mixed * scale).astype(BF16)
    out_ref[...] = jnp.dot(normed_ref[...], w_ref[...], preferred_element_type=F32).astype(BF16)


def handed_on(array):
    size = lax.axis_size("segment")
    return lax.ppermute(array, "segment", [((i - 1) % size, i) for i in range(size)])


def shards(queries, key_rows, value_rows, out_weight):
    q, k, v, w = queries[0], key_rows[0], value_rows[0], out_weight[0]
    rows, width = q.shape
    blocks = lax.axis_size("seq")
    near = [[g * GROUP + m for m in range(GROUP)] for g in range(blocks // GROUP)]
    far = [[g * GROUP + m for g in range(blocks // GROUP)] for m in range(GROUP)]
    piece = (HEADS * HEAD_DIM // GROUP, HEAD_DIM)
    block = pltpu.VMEM((rows, width), BF16)
    sems = lambda n: pltpu.SemaphoreType.DMA((HEADS // SLAB, n))

    states = call(
        states_kernel, jax.ShapeDtypeStruct((HEADS * HEAD_DIM, HEAD_DIM), BF16), (k, v), [ANY] * 2,
        2 * rows * width * HEAD_DIM, 2 * rows * width * 2, limit=60 << 20, scratch=[block, block, sems(2)],
    )
    states_next = handed_on(states)
    pair = call(
        local_kernel, jax.ShapeDtypeStruct((2 * rows, width), BF16), (q, k, v, states), [ANY] * 4,
        4 * rows * rows * width, 5 * rows * width * 2, limit=60 << 20, scratch=[block, block, sems(3)],
    )
    states_next, w, pair = lax.optimization_barrier((states_next, w, pair))
    w_next, pair_next = handed_on(w), handed_on(pair)
    slices = lax.all_to_all(states_next.reshape(GROUP, *piece), "seq", 0, 0, axis_index_groups=near)
    total = call(
        total_kernel, jax.ShapeDtypeStruct(piece, F32), (slices,), [VMEM], 1 << 17, 1 << 19,
    )
    totals = lax.all_gather(total, "seq", axis_index_groups=far)
    group = (lax.axis_index("seq") // GROUP).astype(jnp.int32).reshape(1)
    prefixes = call(
        prefix_kernel, jax.ShapeDtypeStruct((GROUP, *piece), BF16), (group, slices, totals),
        [SMEM, VMEM, VMEM], 1 << 18, 1 << 20,
    )
    carried = lax.all_to_all(prefixes, "seq", 0, 0, axis_index_groups=near).reshape(-1, HEAD_DIM)
    branch = call(
        branch_kernel, jax.ShapeDtypeStruct((rows, width), BF16),
        (pair_next, carried, w_next), [VMEM] * 3,
        2 * rows * width * (width + HEAD_DIM), 6 << 20, scratch=[pltpu.VMEM((rows, width), BF16)],
    )
    return branch[None]


def solution(mesh):
    return jax.shard_map(
        shards,
        mesh=mesh,
        in_specs=(
            P("segment", "seq", None),
            P("segment", "seq", None),
            P("segment", "seq", None),
            P("segment", None, None),
        ),
        out_specs=P("segment", "seq", None),
        check_vma=False,
    )
```

time: 77.2 us -> 71.9 us (0.931)
  waiting for transfers between devices: 28.7 us -> 20.1 us
  Pallas kernels: 5.1 us -> 12.3 us
  local copies, waits for them, and re-layouts: 6.95 us -> 0 us
  starting transfers between devices: 12.2 us -> 15 us
    ppermute x1 -> x3, waiting for transfers between devices: 11.1 us -> 1.06 us  [handed_on(): lax.ppermute(array, 'segment', [((i - 1) % size, i) for i in range(size)])]
    pallas_call x5, Pallas kernels: 5.1 us -> 12.3 us  [call(): pl.pallas_call(body, out_shape=out_shape, in_specs=specs, out_specs=out_s...]
    ppermute x1 -> x3, starting transfers between devices: 0.02 us -> 7 us  [handed_on(): lax.ppermute(array, 'segment', [((i - 1) % size, i) for i in range(size)])]
    unnamed x15 -> x0, local copies, waits for them, and re-layouts: 6.95 us -> none
    all_to_all x1, starting transfers between devices: 8.64 us -> 3.73 us  [shards(): lax.all_to_all(states_next.reshape(GROUP, *piece), 'seq', 0, 0, axis_inde...]
    all_to_all x1, waiting for transfers between devices: 7 us -> 9.97 us  [shards(): lax.all_to_all(prefixes, 'seq', 0, 0, axis_index_groups=near)]
    all_to_all x1, waiting for transfers between devices: 10.7 us -> 9.05 us  [shards(): lax.all_to_all(states_next.reshape(GROUP, *piece), 'seq', 0, 0, axis_inde...]
  transfers between devices with their start and end apart: 3 -> 5, of which waited for: 3 -> 3; matrix products, arithmetic and copies ran while one was open for 0% -> 0% of each run, Pallas kernels for 2% -> 8%
where the time goes in v2:
time: 71.9 us; the launch traced here: 71.2 us
  blocking collectives  23.8 us (33%)
  waiting for transfers between devices  20.1 us (28%)
  starting transfers between devices  15 us (21%)
  Pallas kernels  12.3 us (17%)
    all_gather x1, blocking collectives, shards(): totals = lax.all_gather(total, 'seq', axis_index_groups=far)  23.8 us
    pallas_call x5, Pallas kernels, call(): pl.pallas_call(body, out_shape=out_shape, in_specs=specs, out_specs=out_s...  12.3 us
    all_to_all x1, waiting for transfers between devices, shards(): lax.all_to_all(prefixes, 'seq', 0, 0, axis_index_groups=near)  9.97 us
    all_to_all x1, waiting for transfers between devices, shards(): lax.all_to_all(states_next.reshape(GROUP, *piece), 'seq', 0, 0, axis_inde...  9.05 us
    ppermute x3, starting transfers between devices, handed_on(): lax.ppermute(array, 'segment', [((i - 1) % size, i) for i in range(size)])  7 us
    all_to_all x1, starting transfers between devices, shards(): lax.all_to_all(prefixes, 'seq', 0, 0, axis_index_groups=near)  4.23 us
    all_to_all x1, starting transfers between devices, shards(): lax.all_to_all(states_next.reshape(GROUP, *piece), 'seq', 0, 0, axis_inde...  3.73 us
  transfers between devices with their start and end apart: 5, of which 3 were waited for; matrix products, arithmetic and copies ran while one was open for 0% of the time, Pallas kernels for 8%

profile of v2, /device:TPU:6, one launch (start us, length us, event | category | flops | bytes accessed | tf_op | source)
XLA Modules:
  0.0 71.2 jit_solution(14721272310043591360)
XLA Ops:
  0.0 2.8 %shard_map.46.after_ref = bf16[1024,128]{1,0:T(8,128)(2,1)} custom-call(bf16[368,1024]{1,0:T(8,128)(2,1)} %bitcast.11, bf16[368,1024]{1,0:T(8,128)(2,1)} %bitcast.13), custom_call_target="tpu_custom_call" | custom-call | flops 96468992 | bytes 1507328 | tf_op jit(solution)/shard_map/pallas_call | solution.py:22
  2.9 0.0 collective-permute-start
  2.9 5.0 %shard_map.47 = bf16[736,1024]{1,0:T(8,128)(2,1)} custom-call(bf16[368,1024]{1,0:T(8,128)(2,1)} %bitcast.15, bf16[368,1024]{1,0:T(8,128)(2,1)} %bitcast.12, bf16[368,1024]{1,0:T(8,128)(2,1)} %bitcast.14, bf16[1024,128]{1,0:T(8,128)(2,1)} %shard_map.46.after_ref), custom_call_target="tpu_custom_call" | custom-call | flops 554696704 | bytes 3768320 | tf_op jit(solution)/shard_map/pallas_call | solution.py:22
  7.9 1.1 %collective-permute-done = bf16[1024,128]{1,0:T(8,128)(2,1)} collective-permute-done((bf16[1024,128]{1,0:T(8,128)(2,1)}, bf16[1024,128]{1,0:T(8,128)(2,1)}, u32[]{:S(2)}, u32[]{:S(2)}) %collective-permute-start) | collective-permute-done | bytes 262176 | tf_op jit(solution)/shard_map/ppermute | solution.py:121
  9.0 4.9 %collective-permute-start.2 = (bf16[1024,1024]{1,0:T(8,128)(2,1)}, bf16[1024,1024]{1,0:T(8,128)(2,1)S(1)}, u32[]{:S(2)}, u32[]{:S(2)}) collective-permute-start(bf16[1024,1024]{1,0:T(8,128)(2,1)} %bitcast.16), channel_id=1, source_target_pairs={{7,0},{0,1},{1,2},{2,3},{3,4},{4,5},{5,6},{6,7},{15,8},{8,9},{9,10... | collective-permute-start | bytes 6291464 | tf_op jit(solution)/shard_map/ppermute | solution.py:121
  13.9 3.7 %all-to-all-start = ((bf16[16,64,128]{2,1,0:T(8,128)(2,1)}), bf16[16,64,128]{2,1,0:T(8,128)(2,1)S(1)}, u32[]{:S(2)}, u32[]{:S(2)}) async-start(bf16[16,64,128]{2,1,0:T(8,128)(2,1)} %bitcast.5), calls=%async_computation | async-start | bytes 524288 | tf_op jit(solution)/shard_map/all_to_all | solution.py:145
  17.6 2.1 %collective-permute-start.1 = (bf16[736,1024]{1,0:T(8,128)(2,1)}, bf16[736,1024]{1,0:T(8,128)(2,1)}, u32[]{:S(2)}, u32[]{:S(2)}) collective-permute-start(bf16[736,1024]{1,0:T(8,128)(2,1)} %shard_map.47), channel_id=1, source_target_pairs={{7,0},{0,1},{1,2},{2,3},{3,4},{4,5},{5,6},{6,7},{15,8},{8,9},{9,10... | collective-permute-start | bytes 4521992 | tf_op jit(solution)/shard_map/ppermute | solution.py:121
  19.7 9.1 %all-to-all-done.slices_ref = bf16[16,64,128]{2,1,0:T(8,128)(2,1)S(1)} async-done(((bf16[16,64,128]{2,1,0:T(8,128)(2,1)}), bf16[16,64,128]{2,1,0:T(8,128)(2,1)S(1)}, u32[]{:S(2)}, u32[]{:S(2)}) %all-to-all-start) | async-done | bytes 262176 | tf_op jit(solution)/shard_map/all_to_all | solution.py:145
  28.8 23.8 %all-gather = f32[256,128]{1,0:T(8,128)S(1)} all-gather(f32[64,128]{1,0:T(8,128)S(1)} %shard_map.48), channel_id=2, replica_groups={{0,128,256,384},{8,136,264,392},{16,144,272,400},{24,152,280,408},{32,1..., dimensions={0}, use_global_device_ids=true | all-gather | bytes 163840 | tf_op jit(solution)/shard_map/all_gather | solution.py:149
  52.6 0.8 %shard_map.49 = bf16[16,64,128]{2,1,0:T(8,128)(2,1)} custom-call(s32[1]{0:T(128)} %bitcast.4.group_ref, bf16[16,64,128]{2,1,0:T(8,128)(2,1)S(1)} %all-to-all-done.slices_ref, f32[4,64,128]{2,1,0:T(8,128)S(1)} %bitcast.10), custom_call_target="tpu_custom_call" | custom-call | flops 262144 | bytes 1048576 | tf_op jit(solution)/shard_map/pallas_call | solution.py:22
  53.4 4.2 %all-to-all-start.1 = ((bf16[16,64,128]{2,1,0:T(8,128)(2,1)}), bf16[16,64,128]{2,1,0:T(8,128)(2,1)S(1)}, u32[]{:S(2)}, u32[]{:S(2)}) async-start(bf16[16,64,128]{2,1,0:T(8,128)(2,1)} %shard_map.49), calls=%async_computation.1 | async-start | bytes 524288 | tf_op jit(solution)/shard_map/all_to_all | solution.py:155
  57.6 0.0 collective-permute-done.1.pair_ref
  57.6 10.0 %all-to-all-done.1 = bf16[16,64,128]{2,1,0:T(8,128)(2,1)S(1)} async-done(((bf16[16,64,128]{2,1,0:T(8,128)(2,1)}), bf16[16,64,128]{2,1,0:T(8,128)(2,1)S(1)}, u32[]{:S(2)}, u32[]{:S(2)}) %all-to-all-start.1) | async-done | bytes 262176 | tf_op jit(solution)/shard_map/all_to_all | solution.py:155
  67.6 0.0 collective-permute-done.2.w_ref
  67.6 3.6 %shard_map.50 = bf16[368,1024]{1,0:T(8,128)(2,1)} custom-call(bf16[736,1024]{1,0:T(8,128)(2,1)} %collective-permute-done.1.pair_ref, bf16[1024,128]{1,0:T(8,128)(2,1)S(1)} %bitcast.9, bf16[1024,1024]{1,0:T(8,128)(2,1)S(1)} %collective-permute-done.2.w_ref), custom_call_target="tpu_custom_call" | custom-call | flops 868220928 | bytes 6291456 | tf_op jit(solution)/shard_map/pallas_call | solution.py:22
  (1 shorter events, 0.0 us)
Async XLA Ops:
  2.9 6.1 %collective-permute-start = (bf16[1024,128]{1,0:T(8,128)(2,1)}, bf16[1024,128]{1,0:T(8,128)(2,1)}, u32[]{:S(2)}, u32[]{:S(2)}) collective-permute-start(bf16[1024,128]{1,0:T(8,128)(2,1)} %shard_map.46.after_ref), channel_id=1, source_target_pairs={{7,0},{0,1},{1,2},{2,3},{3,4},{4,5},{5,6},{6,7},{15,8},{8,9},{9,10... | collective-permute-start | bytes 786440 | tf_op jit(solution)/shard_map/ppermute | solution.py:121
  9.0 58.6 %collective-permute-start.2 = (bf16[1024,1024]{1,0:T(8,128)(2,1)}, bf16[1024,1024]{1,0:T(8,128)(2,1)S(1)}, u32[]{:S(2)}, u32[]{:S(2)}) collective-permute-start(bf16[1024,1024]{1,0:T(8,128)(2,1)} %bitcast.16), channel_id=1, source_target_pairs={{7,0},{0,1},{1,2},{2,3},{3,4},{4,5},{5,6},{6,7},{15,8},{8,9},{9,10... | collective-permute-start | bytes 6291464 | tf_op jit(solution)/shard_map/ppermute | solution.py:121
  13.9 14.9 %all-to-all-start = ((bf16[16,64,128]{2,1,0:T(8,128)(2,1)}), bf16[16,64,128]{2,1,0:T(8,128)(2,1)S(1)}, u32[]{:S(2)}, u32[]{:S(2)}) async-start(bf16[16,64,128]{2,1,0:T(8,128)(2,1)} %bitcast.5), calls=%async_computation | async-start | bytes 524288 | tf_op jit(solution)/shard_map/all_to_all | solution.py:145
  17.6 40.0 %collective-permute-start.1 = (bf16[736,1024]{1,0:T(8,128)(2,1)}, bf16[736,1024]{1,0:T(8,128)(2,1)}, u32[]{:S(2)}, u32[]{:S(2)}) collective-permute-start(bf16[736,1024]{1,0:T(8,128)(2,1)} %shard_map.47), channel_id=1, source_target_pairs={{7,0},{0,1},{1,2},{2,3},{3,4},{4,5},{5,6},{6,7},{15,8},{8,9},{9,10... | collective-permute-start | bytes 4521992 | tf_op jit(solution)/shard_map/ppermute | solution.py:121
  53.4 14.2 %all-to-all-start.1 = ((bf16[16,64,128]{2,1,0:T(8,128)(2,1)}), bf16[16,64,128]{2,1,0:T(8,128)(2,1)S(1)}, u32[]{:S(2)}, u32[]{:S(2)}) async-start(bf16[16,64,128]{2,1,0:T(8,128)(2,1)} %shard_map.49), calls=%async_computation.1 | async-start | bytes 524288 | tf_op jit(solution)/shard_map/all_to_all | solution.py:155

commit v3 on v2

--- a/solution.py
+++ b/solution.py
@@ -8,7 +8,7 @@
 HEADS = 8
 HEAD_DIM = 128
 GROUP = 16
-SLAB = 2
+SLAB = 4
 EPSILON = 1e-06
 
 F32 = jnp.float32
@@ -95,17 +95,29 @@
     out_ref[...] = acc
 
 
-def prefix_kernel(group_ref, slices_ref, totals_ref, out_ref):
-    group = group_ref[0]
-    acc = jnp.zeros(out_ref.shape[1:], F32)
-    for g in range(totals_ref.shape[0] - 1):
-        acc = acc + jnp.where(g < group, totals_ref[g], 0.0)
+def prefix_kernel(slices_ref, *refs):
+    totals, out_ref = refs[:-1], refs[-1]
+    acc = totals[0][...]
+    for total in totals[1:]:
+        acc = acc + total[...]
     for m in range(slices_ref.shape[0]):
         out_ref[m] = acc.astype(BF16)
         acc = acc + slices_ref[m].astype(F32)
 
 
-def branch_kernel(pair_ref, carried_ref, w_ref, out_ref, normed_ref):
+def fetch_kernel(pair_hbm, out_ref, sem):
+    copy = pltpu.make_async_copy(pair_hbm, out_ref, sem.at[0])
+    copy.start()
+    copy.wait()
+
+
+def branch_kernel(pair_ref, carried_ref, w_hbm, out_hbm, normed_ref, out_ref, w_ref, w_sem, sem):
+    w_copies = [
+        pltpu.make_async_copy(w_hbm.at[head(h), :], w_ref.at[head(h), :], w_sem.at[h])
+        for h in range(HEADS)
+    ]
+    for copy in w_copies:
+        copy.start()
     rows = out_ref.shape[0]
     for h in range(HEADS):
         mixed = pair_ref[rows : 2 * rows, head(h)].astype(F32) + jnp.dot(
@@ -113,7 +125,19 @@
         )
         scale = lax.rsqrt(jnp.mean(mixed * mixed, axis=1, keepdims=True) + EPSILON)
         normed_ref[:, head(h)] = (mixed * scale).astype(BF16)
-    out_ref[...] = jnp.dot(normed_ref[...], w_ref[...], preferred_element_type=F32).astype(BF16)
+    for copy in w_copies:
+        copy.wait()
+    middle = (rows // 2 + 15) // 16 * 16
+    copies = []
+    for n, (low, high) in enumerate(((0, middle), (middle, rows))):
+        part = pl.ds(low, high - low)
+        out_ref[part, :] = jnp.dot(
+            normed_ref[part, :], w_ref[...], preferred_element_type=F32
+        ).astype(BF16)
+        copies.append(pltpu.make_async_copy(out_ref.at[part], out_hbm.at[part], sem.at[n]))
+        copies[n].start()
+    for copy in copies:
+        copy.wait()
 
 
 def handed_on(array):
@@ -126,7 +150,6 @@
     rows, width = q.shape
     blocks = lax.axis_size("seq")
     near = [[g * GROUP + m for m in range(GROUP)] for g in range(blocks // GROUP)]
-    far = [[g * GROUP + m for g in range(blocks // GROUP)] for m in range(GROUP)]
     piece = (HEADS * HEAD_DIM // GROUP, HEAD_DIM)
     block = pltpu.VMEM((rows, width), BF16)
     sems = lambda n: pltpu.SemaphoreType.DMA((HEADS // SLAB, n))
@@ -144,19 +167,29 @@
     w_next, pair_next = handed_on(w), handed_on(pair)
     slices = lax.all_to_all(states_next.reshape(GROUP, *piece), "seq", 0, 0, axis_index_groups=near)
     total = call(
-        total_kernel, jax.ShapeDtypeStruct(piece, F32), (slices,), [VMEM], 1 << 17, 1 << 19,
-    )
-    totals = lax.all_gather(total, "seq", axis_index_groups=far)
-    group = (lax.axis_index("seq") // GROUP).astype(jnp.int32).reshape(1)
+        total_kernel, jax.ShapeDtypeStruct(piece, F32), (slices,), [VMEM], 1 << 17, 1 << 19, limit=4 << 20,
+    )
+    totals = [
+        lax.ppermute(total, "seq", [(i, i + d * GROUP) for i in range(blocks - d * GROUP)])
+        for d in range(1, blocks // GROUP)
+    ]
     prefixes = call(
-        prefix_kernel, jax.ShapeDtypeStruct((GROUP, *piece), BF16), (group, slices, totals),
-        [SMEM, VMEM, VMEM], 1 << 18, 1 << 20,
+        prefix_kernel, jax.ShapeDtypeStruct((GROUP, *piece), BF16), (slices, *totals),
+        [VMEM] * (1 + len(totals)), 1 << 18, 1 << 20, limit=4 << 20,
     )
     carried = lax.all_to_all(prefixes, "seq", 0, 0, axis_index_groups=near).reshape(-1, HEAD_DIM)
+    pair_next = call(
+        fetch_kernel, jax.ShapeDtypeStruct((2 * rows, width), BF16), (pair_next,), [ANY],
+        0, 4 * rows * width, limit=8 << 20, scratch=[pltpu.SemaphoreType.DMA((1,))],
+    )
     branch = call(
         branch_kernel, jax.ShapeDtypeStruct((rows, width), BF16),
-        (pair_next, carried, w_next), [VMEM] * 3,
-        2 * rows * width * (width + HEAD_DIM), 6 << 20, scratch=[pltpu.VMEM((rows, width), BF16)],
+        (pair_next, carried, w_next), [VMEM, VMEM, ANY],
+        2 * rows * width * (width + HEAD_DIM), 6 << 20, out_specs=ANY, limit=16 << 20,
+        scratch=[
+            block, block, pltpu.VMEM((width, width), BF16),
+            pltpu.SemaphoreType.DMA((HEADS,)), pltpu.SemaphoreType.DMA((2,)),
+        ],
     )
     return branch[None]
 

time: 71.9 us -> 69.2 us (0.962)
  blocking collectives: 23.8 us -> 0 us
  starting transfers between devices: 15 us -> 34.9 us
  waiting for transfers between devices: 20.1 us -> 21.8 us
    all_gather x1 -> x0, blocking collectives: 23.8 us -> none  [shards(): totals = lax.all_gather(total, 'seq', axis_index_groups=far)]
    ppermute x0 -> x3, starting transfers between devices: none -> 19.1 us  [shards(): lax.ppermute(total, 'seq', [(i, i + d * GROUP) for i in range(blocks - d...]
    ppermute x0 -> x3, waiting for transfers between devices: none -> 1.56 us  [shards(): lax.ppermute(total, 'seq', [(i, i + d * GROUP) for i in range(blocks - d...]
    all_to_all x1, starting transfers between devices: 4.23 us -> 5.08 us  [shards(): lax.all_to_all(prefixes, 'seq', 0, 0, axis_index_groups=near)]
    pallas_call x5 -> x6, Pallas kernels: 12.3 us -> 12 us  [call(): pl.pallas_call(body, out_shape=out_shape, in_specs=specs, out_specs=out_s...]
  transfers between devices with their start and end apart: 5 -> 8, of which waited for: 3 -> 4; matrix products, arithmetic and copies ran while one was open for 0% -> 0% of each run, Pallas kernels for 8% -> 8%
where the time goes in v3:
time: 69.2 us; the launch traced here: 68.8 us
  starting transfers between devices  34.9 us (50%)
  waiting for transfers between devices  21.8 us (32%)
  Pallas kernels  12 us (17%)
    ppermute x3, starting transfers between devices, shards(): lax.ppermute(total, 'seq', [(i, i + d * GROUP) for i in range(blocks - d...  19.1 us
    pallas_call x6, Pallas kernels, call(): pl.pallas_call(body, out_shape=out_shape, in_specs=specs, out_specs=out_s...  12 us
    all_to_all x1, waiting for transfers between devices, shards(): lax.all_to_all(prefixes, 'seq', 0, 0, axis_index_groups=near)  9.61 us
    all_to_all x1, waiting for transfers between devices, shards(): lax.all_to_all(states_next.reshape(GROUP, *piece), 'seq', 0, 0, axis_inde...  9.04 us
    ppermute x3, starting transfers between devices, handed_on(): lax.ppermute(array, 'segment', [((i - 1) % size, i) for i in range(size)])  6.5 us
    all_to_all x1, starting transfers between devices, shards(): lax.all_to_all(prefixes, 'seq', 0, 0, axis_index_groups=near)  5.08 us
    all_to_all x1, starting transfers between devices, shards(): lax.all_to_all(states_next.reshape(GROUP, *piece), 'seq', 0, 0, axis_inde...  4.24 us
    ppermute x3, waiting for transfers between devices, handed_on(): lax.ppermute(array, 'segment', [((i - 1) % size, i) for i in range(size)])  1.57 us
  transfers between devices with their start and end apart: 8, of which 4 were waited for; matrix products, arithmetic and copies ran while one was open for 0% of the time, Pallas kernels for 8%

profile of v3, /device:TPU:6, one launch (start us, length us, event | category | flops | bytes accessed | tf_op | source)
XLA Modules:
  0.0 68.8 jit_solution(14178348320015516758)
XLA Ops:
  0.0 2.5 %shard_map.46.after_ref = bf16[1024,128]{1,0:T(8,128)(2,1)} custom-call(bf16[368,1024]{1,0:T(8,128)(2,1)} %bitcast.8, bf16[368,1024]{1,0:T(8,128)(2,1)} %bitcast.10), custom_call_target="tpu_custom_call" | custom-call | flops 96468992 | bytes 1507328 | tf_op jit(solution)/shard_map/pallas_call | solution.py:22
  2.5 0.0 collective-permute-start
  2.5 4.5 %shard_map.47 = bf16[736,1024]{1,0:T(8,128)(2,1)} custom-call(bf16[368,1024]{1,0:T(8,128)(2,1)} %bitcast.12, bf16[368,1024]{1,0:T(8,128)(2,1)} %bitcast.9, bf16[368,1024]{1,0:T(8,128)(2,1)} %bitcast.11, bf16[1024,128]{1,0:T(8,128)(2,1)} %shard_map.46.after_ref), custom_call_target="tpu_custom_call" | custom-call | flops 554696704 | bytes 3768320 | tf_op jit(solution)/shard_map/pallas_call | solution.py:22
  7.0 1.6 %collective-permute-done = bf16[1024,128]{1,0:T(8,128)(2,1)} collective-permute-done((bf16[1024,128]{1,0:T(8,128)(2,1)}, bf16[1024,128]{1,0:T(8,128)(2,1)}, u32[]{:S(2)}, u32[]{:S(2)}) %collective-permute-start) | collective-permute-done | bytes 262176 | tf_op jit(solution)/shard_map/ppermute | solution.py:145
  8.6 4.4 %collective-permute-start.5 = (bf16[1024,1024]{1,0:T(8,128)(2,1)}, bf16[1024,1024]{1,0:T(8,128)(2,1)}, u32[]{:S(2)}, u32[]{:S(2)}) collective-permute-start(bf16[1024,1024]{1,0:T(8,128)(2,1)} %bitcast.2), channel_id=1, source_target_pairs={{7,0},{0,1},{1,2},{2,3},{3,4},{4,5},{5,6},{6,7},{15,8},{8,9},{9,10... | collective-permute-start | bytes 6291464 | tf_op jit(solution)/shard_map/ppermute | solution.py:145
  13.0 4.2 %all-to-all-start = ((bf16[16,64,128]{2,1,0:T(8,128)(2,1)}), bf16[16,64,128]{2,1,0:T(8,128)(2,1)S(1)}, u32[]{:S(2)}, u32[]{:S(2)}) async-start(bf16[16,64,128]{2,1,0:T(8,128)(2,1)} %bitcast.4), calls=%async_computation | async-start | bytes 524288 | tf_op jit(solution)/shard_map/all_to_all | solution.py:168
  17.3 2.1 %collective-permute-start.1 = (bf16[736,1024]{1,0:T(8,128)(2,1)}, bf16[736,1024]{1,0:T(8,128)(2,1)S(1)}, u32[]{:S(2)}, u32[]{:S(2)}) collective-permute-start(bf16[736,1024]{1,0:T(8,128)(2,1)} %shard_map.47), channel_id=1, source_target_pairs={{7,0},{0,1},{1,2},{2,3},{3,4},{4,5},{5,6},{6,7},{15,8},{8,9},{9,10... | collective-permute-start | bytes 4521992 | tf_op jit(solution)/shard_map/ppermute | solution.py:145
  19.3 9.0 %all-to-all-done.slices_ref = bf16[16,64,128]{2,1,0:T(8,128)(2,1)S(1)} async-done(((bf16[16,64,128]{2,1,0:T(8,128)(2,1)}), bf16[16,64,128]{2,1,0:T(8,128)(2,1)S(1)}, u32[]{:S(2)}, u32[]{:S(2)}) %all-to-all-start) | async-done | bytes 262176 | tf_op jit(solution)/shard_map/all_to_all | solution.py:168
  28.4 10.5 %collective-permute-start.4 = (f32[64,128]{1,0:T(8,128)S(1)}, f32[64,128]{1,0:T(8,128)S(1)}, u32[]{:S(2)}, u32[]{:S(2)}) collective-permute-start(f32[64,128]{1,0:T(8,128)S(1)} %shard_map.49), channel_id=1, source_target_pairs={{0,384},{8,392},{16,400},{24,408},{32,416},{40,424},{48,432},{56,4... | collective-permute-start | bytes 98312 | tf_op jit(solution)/shard_map/ppermute | solution.py:173
  39.0 3.6 %collective-permute-start.3 = (f32[64,128]{1,0:T(8,128)S(1)}, f32[64,128]{1,0:T(8,128)S(1)}, u32[]{:S(2)}, u32[]{:S(2)}) collective-permute-start(f32[64,128]{1,0:T(8,128)S(1)} %shard_map.49), channel_id=1, source_target_pairs={{0,256},{8,264},{16,272},{24,280},{32,288},{40,296},{48,304},{56,3... | collective-permute-start | bytes 98312 | tf_op jit(solution)/shard_map/ppermute | solution.py:173
  42.6 4.9 %collective-permute-start.2 = (f32[64,128]{1,0:T(8,128)S(1)}, f32[64,128]{1,0:T(8,128)S(1)}, u32[]{:S(2)}, u32[]{:S(2)}) collective-permute-start(f32[64,128]{1,0:T(8,128)S(1)} %shard_map.49), channel_id=1, source_target_pairs={{0,128},{8,136},{16,144},{24,152},{32,160},{40,168},{48,176},{56,1... | collective-permute-start | bytes 98312 | tf_op jit(solution)/shard_map/ppermute | solution.py:173
  47.5 0.0 collective-permute-done.4.refs_2_
  47.5 0.0 collective-permute-done.3.refs_1_
  47.6 1.6 %collective-permute-done.2.refs_0_ = f32[64,128]{1,0:T(8,128)S(1)} collective-permute-done((f32[64,128]{1,0:T(8,128)S(1)}, f32[64,128]{1,0:T(8,128)S(1)}, u32[]{:S(2)}, u32[]{:S(2)}) %collective-permute-start.2) | collective-permute-done | bytes 32800 | tf_op jit(solution)/shard_map/ppermute | solution.py:173
  49.1 0.7 %shard_map.50 = bf16[16,64,128]{2,1,0:T(8,128)(2,1)} custom-call(bf16[16,64,128]{2,1,0:T(8,128)(2,1)S(1)} %all-to-all-done.slices_ref, f32[64,128]{1,0:T(8,128)S(1)} %collective-permute-done.2.refs_0_, f32[64,128]{1,0:T(8,128)S(1)} %collective-permute-done.3.refs_1_, f32[64,128]{1,0:T(8,128)S(1)} %collective-permute-done.4.refs_2_), custom_call_target="tpu_custom_call" | custom-call | flops 262144 | bytes 1048576 | tf_op jit(solution)/shard_map/pallas_call | solution.py:22
  49.9 5.1 %all-to-all-start.1 = ((bf16[16,64,128]{2,1,0:T(8,128)(2,1)}), bf16[16,64,128]{2,1,0:T(8,128)(2,1)S(1)}, u32[]{:S(2)}, u32[]{:S(2)}) async-start(bf16[16,64,128]{2,1,0:T(8,128)(2,1)} %shard_map.50), calls=%async_computation.1 | async-start | bytes 524288 | tf_op jit(solution)/shard_map/all_to_all | solution.py:180
  55.0 0.0 collective-permute-done.1.pair_hbm
  55.0 0.4 shard_map.48.pair_ref
  55.3 9.6 %all-to-all-done.1 = bf16[16,64,128]{2,1,0:T(8,128)(2,1)S(1)} async-done(((bf16[16,64,128]{2,1,0:T(8,128)(2,1)}), bf16[16,64,128]{2,1,0:T(8,128)(2,1)S(1)}, u32[]{:S(2)}, u32[]{:S(2)}) %all-to-all-start.1) | async-done | bytes 262176 | tf_op jit(solution)/shard_map/all_to_all | solution.py:180
  64.9 0.0 collective-permute-done.5.w_hbm
  64.9 3.8 %shard_map.51 = bf16[368,1024]{1,0:T(8,128)(2,1)} custom-call(bf16[736,1024]{1,0:T(8,128)(2,1)S(1)} %shard_map.48.pair_ref, bf16[1024,128]{1,0:T(8,128)(2,1)S(1)} %bitcast.7, bf16[1024,1024]{1,0:T(8,128)(2,1)} %collective-permute-done.5.w_hbm), custom_call_target="tpu_custom_call" | custom-call | flops 868220928 | bytes 6291456 | tf_op jit(solution)/shard_map/pallas_call | solution.py:22
  (1 shorter events, 0.0 us)
Async XLA Ops:
  2.5 6.1 %collective-permute-start = (bf16[1024,128]{1,0:T(8,128)(2,1)}, bf16[1024,128]{1,0:T(8,128)(2,1)}, u32[]{:S(2)}, u32[]{:S(2)}) collective-permute-start(bf16[1024,128]{1,0:T(8,128)(2,1)} %shard_map.46.after_ref), channel_id=1, source_target_pairs={{7,0},{0,1},{1,2},{2,3},{3,4},{4,5},{5,6},{6,7},{15,8},{8,9},{9,10... | collective-permute-start | bytes 786440 | tf_op jit(solution)/shard_map/ppermute | solution.py:145
  8.6 56.3 %collective-permute-start.5 = (bf16[1024,1024]{1,0:T(8,128)(2,1)}, bf16[1024,1024]{1,0:T(8,128)(2,1)}, u32[]{:S(2)}, u32[]{:S(2)}) collective-permute-start(bf16[1024,1024]{1,0:T(8,128)(2,1)} %bitcast.2), channel_id=1, source_target_pairs={{7,0},{0,1},{1,2},{2,3},{3,4},{4,5},{5,6},{6,7},{15,8},{8,9},{9,10... | collective-permute-start | bytes 6291464 | tf_op jit(solution)/shard_map/ppermute | solution.py:145
  13.0 15.4 %all-to-all-start = ((bf16[16,64,128]{2,1,0:T(8,128)(2,1)}), bf16[16,64,128]{2,1,0:T(8,128)(2,1)S(1)}, u32[]{:S(2)}, u32[]{:S(2)}) async-start(bf16[16,64,128]{2,1,0:T(8,128)(2,1)} %bitcast.4), calls=%async_computation | async-start | bytes 524288 | tf_op jit(solution)/shard_map/all_to_all | solution.py:168
  17.3 37.7 %collective-permute-start.1 = (bf16[736,1024]{1,0:T(8,128)(2,1)}, bf16[736,1024]{1,0:T(8,128)(2,1)S(1)}, u32[]{:S(2)}, u32[]{:S(2)}) collective-permute-start(bf16[736,1024]{1,0:T(8,128)(2,1)} %shard_map.47), channel_id=1, source_target_pairs={{7,0},{0,1},{1,2},{2,3},{3,4},{4,5},{5,6},{6,7},{15,8},{8,9},{9,10... | collective-permute-start | bytes 4521992 | tf_op jit(solution)/shard_map/ppermute | solution.py:145
  28.4 19.1 %collective-permute-start.4 = (f32[64,128]{1,0:T(8,128)S(1)}, f32[64,128]{1,0:T(8,128)S(1)}, u32[]{:S(2)}, u32[]{:S(2)}) collective-permute-start(f32[64,128]{1,0:T(8,128)S(1)} %shard_map.49), channel_id=1, source_target_pairs={{0,384},{8,392},{16,400},{24,408},{32,416},{40,424},{48,432},{56,4... | collective-permute-start | bytes 98312 | tf_op jit(solution)/shard_map/ppermute | solution.py:173
  39.0 8.6 %collective-permute-start.3 = (f32[64,128]{1,0:T(8,128)S(1)}, f32[64,128]{1,0:T(8,128)S(1)}, u32[]{:S(2)}, u32[]{:S(2)}) collective-permute-start(f32[64,128]{1,0:T(8,128)S(1)} %shard_map.49), channel_id=1, source_target_pairs={{0,256},{8,264},{16,272},{24,280},{32,288},{40,296},{48,304},{56,3... | collective-permute-start | bytes 98312 | tf_op jit(solution)/shard_map/ppermute | solution.py:173
  42.6 6.5 %collective-permute-start.2 = (f32[64,128]{1,0:T(8,128)S(1)}, f32[64,128]{1,0:T(8,128)S(1)}, u32[]{:S(2)}, u32[]{:S(2)}) collective-permute-start(f32[64,128]{1,0:T(8,128)S(1)} %shard_map.49), channel_id=1, source_target_pairs={{0,128},{8,136},{16,144},{24,152},{32,160},{40,168},{48,176},{56,1... | collective-permute-start | bytes 98312 | tf_op jit(solution)/shard_map/ppermute | solution.py:173
  49.9 15.1 %all-to-all-start.1 = ((bf16[16,64,128]{2,1,0:T(8,128)(2,1)}), bf16[16,64,128]{2,1,0:T(8,128)(2,1)S(1)}, u32[]{:S(2)}, u32[]{:S(2)}) async-start(bf16[16,64,128]{2,1,0:T(8,128)(2,1)} %shard_map.50), calls=%async_computation.1 | async-start | bytes 524288 | tf_op jit(solution)/shard_map/all_to_all | solution.py:180

commit v4 on v3

--- a/solution.py
+++ b/solution.py
@@ -105,28 +105,23 @@
         acc = acc + slices_ref[m].astype(F32)
 
 
-def fetch_kernel(pair_hbm, out_ref, sem):
-    copy = pltpu.make_async_copy(pair_hbm, out_ref, sem.at[0])
-    copy.start()
-    copy.wait()
-
-
-def branch_kernel(pair_ref, carried_ref, w_hbm, out_hbm, normed_ref, out_ref, w_ref, w_sem, sem):
-    w_copies = [
-        pltpu.make_async_copy(w_hbm.at[head(h), :], w_ref.at[head(h), :], w_sem.at[h])
-        for h in range(HEADS)
-    ]
-    for copy in w_copies:
-        copy.start()
+def branch_kernel(pair_hbm, carried_ref, w_ref, out_hbm, q_ref, local_ref, normed_ref, out_ref, in_sem, sem):
     rows = out_ref.shape[0]
+    in_copies = slab_copies(
+        (pair_hbm.at[pl.ds(0, rows)], pair_hbm.at[pl.ds(rows, rows)]), (q_ref, local_ref), in_sem
+    )
+    for slab in in_copies:
+        for copy in slab:
+            copy.start()
     for h in range(HEADS):
-        mixed = pair_ref[rows : 2 * rows, head(h)].astype(F32) + jnp.dot(
-            pair_ref[0:rows, head(h)], carried_ref[head(h), :], preferred_element_type=F32
+        if h % SLAB == 0:
+            for copy in in_copies[h // SLAB]:
+                copy.wait()
+        mixed = local_ref[:, head(h)].astype(F32) + jnp.dot(
+            q_ref[:, head(h)], carried_ref[head(h), :], preferred_element_type=F32
         )
         scale = lax.rsqrt(jnp.mean(mixed * mixed, axis=1, keepdims=True) + EPSILON)
         normed_ref[:, head(h)] = (mixed * scale).astype(BF16)
-    for copy in w_copies:
-        copy.wait()
     middle = (rows // 2 + 15) // 16 * 16
     copies = []
     for n, (low, high) in enumerate(((0, middle), (middle, rows))):
@@ -169,27 +164,21 @@
     total = call(
         total_kernel, jax.ShapeDtypeStruct(piece, F32), (slices,), [VMEM], 1 << 17, 1 << 19, limit=4 << 20,
     )
+    groups = blocks // GROUP
+    order = sorted(range(1, groups), key=lambda d: min(d, groups - d))
     totals = [
         lax.ppermute(total, "seq", [(i, i + d * GROUP) for i in range(blocks - d * GROUP)])
-        for d in range(1, blocks // GROUP)
+        for d in order
     ]
     prefixes = call(
         prefix_kernel, jax.ShapeDtypeStruct((GROUP, *piece), BF16), (slices, *totals),
         [VMEM] * (1 + len(totals)), 1 << 18, 1 << 20, limit=4 << 20,
     )
     carried = lax.all_to_all(prefixes, "seq", 0, 0, axis_index_groups=near).reshape(-1, HEAD_DIM)
-    pair_next = call(
-        fetch_kernel, jax.ShapeDtypeStruct((2 * rows, width), BF16), (pair_next,), [ANY],
-        0, 4 * rows * width, limit=8 << 20, scratch=[pltpu.SemaphoreType.DMA((1,))],
-    )
     branch = call(
-        branch_kernel, jax.ShapeDtypeStruct((rows, width), BF16),
-        (pair_next, carried, w_next), [VMEM, VMEM, ANY],
+        branch_kernel, jax.ShapeDtypeStruct((rows, width), BF16), (pair_next, carried, w_next), [ANY, VMEM, VMEM],
         2 * rows * width * (width + HEAD_DIM), 6 << 20, out_specs=ANY, limit=16 << 20,
-        scratch=[
-            block, block, pltpu.VMEM((width, width), BF16),
-            pltpu.SemaphoreType.DMA((HEADS,)), pltpu.SemaphoreType.DMA((2,)),
-        ],
+        scratch=[block, block, block, block, sems(2), pltpu.SemaphoreType.DMA((2,))],
     )
     return branch[None]
 

time: 69.2 us -> 68.2 us (0.986)
  Pallas kernels: 12 us -> 11.3 us
    pallas_call x6 -> x5, Pallas kernels: 12 us -> 11.3 us  [call(): pl.pallas_call(body, out_shape=out_shape, in_specs=specs, out_specs=out_s...]
  transfers between devices with their start and end apart: 8 -> 8, of which waited for: 4 -> 5; matrix products, arithmetic and copies ran while one was open for 0% -> 0% of each run, Pallas kernels for 8% -> 8%
where the time goes in v4:
time: 68.2 us; the launch traced here: 67.8 us
  starting transfers between devices  34.3 us (50%)
  waiting for transfers between devices  22.1 us (32%)
  Pallas kernels  11.3 us (17%)
    ppermute x3, starting transfers between devices, shards(): lax.ppermute(total, 'seq', [(i, i + d * GROUP) for i in range(blocks - d...  18.5 us
    pallas_call x5, Pallas kernels, call(): pl.pallas_call(body, out_shape=out_shape, in_specs=specs, out_specs=out_s...  11.3 us
    all_to_all x1, waiting for transfers between devices, shards(): lax.all_to_all(prefixes, 'seq', 0, 0, axis_index_groups=near)  9.97 us
    all_to_all x1, waiting for transfers between devices, shards(): lax.all_to_all(states_next.reshape(GROUP, *piece), 'seq', 0, 0, axis_inde...  9.04 us
    ppermute x3, starting transfers between devices, handed_on(): lax.ppermute(array, 'segment', [((i - 1) % size, i) for i in range(size)])  6.52 us
    all_to_all x1, starting transfers between devices, shards(): lax.all_to_all(prefixes, 'seq', 0, 0, axis_index_groups=near)  5.08 us
    all_to_all x1, starting transfers between devices, shards(): lax.all_to_all(states_next.reshape(GROUP, *piece), 'seq', 0, 0, axis_inde...  4.21 us
    ppermute x3, waiting for transfers between devices, shards(): lax.ppermute(total, 'seq', [(i, i + d * GROUP) for i in range(blocks - d...  1.57 us
  transfers between devices with their start and end apart: 8, of which 5 were waited for; matrix products, arithmetic and copies ran while one was open for 0% of the time, Pallas kernels for 8%

profile of v4, /device:TPU:6, one launch (start us, length us, event | category | flops | bytes accessed | tf_op | source)
XLA Modules:
  0.0 67.8 jit_solution(2221420009580302875)
XLA Ops:
  0.0 2.5 %shard_map.46.after_ref = bf16[1024,128]{1,0:T(8,128)(2,1)} custom-call(bf16[368,1024]{1,0:T(8,128)(2,1)} %bitcast.8, bf16[368,1024]{1,0:T(8,128)(2,1)} %bitcast.10), custom_call_target="tpu_custom_call" | custom-call | flops 96468992 | bytes 1507328 | tf_op jit(solution)/shard_map/pallas_call | solution.py:22
  2.5 0.0 collective-permute-start
  2.5 4.6 %shard_map.47 = bf16[736,1024]{1,0:T(8,128)(2,1)} custom-call(bf16[368,1024]{1,0:T(8,128)(2,1)} %bitcast.12, bf16[368,1024]{1,0:T(8,128)(2,1)} %bitcast.9, bf16[368,1024]{1,0:T(8,128)(2,1)} %bitcast.11, bf16[1024,128]{1,0:T(8,128)(2,1)} %shard_map.46.after_ref), custom_call_target="tpu_custom_call" | custom-call | flops 554696704 | bytes 3768320 | tf_op jit(solution)/shard_map/pallas_call | solution.py:22
  7.1 1.5 %collective-permute-done = bf16[1024,128]{1,0:T(8,128)(2,1)} collective-permute-done((bf16[1024,128]{1,0:T(8,128)(2,1)}, bf16[1024,128]{1,0:T(8,128)(2,1)}, u32[]{:S(2)}, u32[]{:S(2)}) %collective-permute-start) | collective-permute-done | bytes 262176 | tf_op jit(solution)/shard_map/ppermute | solution.py:140
  8.6 4.4 %collective-permute-start.5 = (bf16[1024,1024]{1,0:T(8,128)(2,1)}, bf16[1024,1024]{1,0:T(8,128)(2,1)S(1)}, u32[]{:S(2)}, u32[]{:S(2)}) collective-permute-start(bf16[1024,1024]{1,0:T(8,128)(2,1)} %bitcast.13), channel_id=1, source_target_pairs={{7,0},{0,1},{1,2},{2,3},{3,4},{4,5},{5,6},{6,7},{15,8},{8,9},{9,10... | collective-permute-start | bytes 6291464 | tf_op jit(solution)/shard_map/ppermute | solution.py:140
  13.0 4.2 %all-to-all-start = ((bf16[16,64,128]{2,1,0:T(8,128)(2,1)}), bf16[16,64,128]{2,1,0:T(8,128)(2,1)S(1)}, u32[]{:S(2)}, u32[]{:S(2)}) async-start(bf16[16,64,128]{2,1,0:T(8,128)(2,1)} %bitcast.4), calls=%async_computation | async-start | bytes 524288 | tf_op jit(solution)/shard_map/all_to_all | solution.py:163
  17.3 2.1 %collective-permute-start.1 = (bf16[736,1024]{1,0:T(8,128)(2,1)}, bf16[736,1024]{1,0:T(8,128)(2,1)}, u32[]{:S(2)}, u32[]{:S(2)}) collective-permute-start(bf16[736,1024]{1,0:T(8,128)(2,1)} %shard_map.47), channel_id=1, source_target_pairs={{7,0},{0,1},{1,2},{2,3},{3,4},{4,5},{5,6},{6,7},{15,8},{8,9},{9,10... | collective-permute-start | bytes 4521992 | tf_op jit(solution)/shard_map/ppermute | solution.py:140
  19.3 9.0 %all-to-all-done.slices_ref = bf16[16,64,128]{2,1,0:T(8,128)(2,1)S(1)} async-done(((bf16[16,64,128]{2,1,0:T(8,128)(2,1)}), bf16[16,64,128]{2,1,0:T(8,128)(2,1)S(1)}, u32[]{:S(2)}, u32[]{:S(2)}) %all-to-all-start) | async-done | bytes 262176 | tf_op jit(solution)/shard_map/all_to_all | solution.py:163
  28.4 13.5 %collective-permute-start.4 = (f32[64,128]{1,0:T(8,128)S(1)}, f32[64,128]{1,0:T(8,128)S(1)}, u32[]{:S(2)}, u32[]{:S(2)}) collective-permute-start(f32[64,128]{1,0:T(8,128)S(1)} %shard_map.48), channel_id=1, source_target_pairs={{0,256},{8,264},{16,272},{24,280},{32,288},{40,296},{48,304},{56,3... | collective-permute-start | bytes 98312 | tf_op jit(solution)/shard_map/ppermute | solution.py:170
  41.9 1.3 %collective-permute-start.3 = (f32[64,128]{1,0:T(8,128)S(1)}, f32[64,128]{1,0:T(8,128)S(1)}, u32[]{:S(2)}, u32[]{:S(2)}) collective-permute-start(f32[64,128]{1,0:T(8,128)S(1)} %shard_map.48), channel_id=1, source_target_pairs={{0,384},{8,392},{16,400},{24,408},{32,416},{40,424},{48,432},{56,4... | collective-permute-start | bytes 98312 | tf_op jit(solution)/shard_map/ppermute | solution.py:170
  43.2 3.7 %collective-permute-start.2 = (f32[64,128]{1,0:T(8,128)S(1)}, f32[64,128]{1,0:T(8,128)S(1)}, u32[]{:S(2)}, u32[]{:S(2)}) collective-permute-start(f32[64,128]{1,0:T(8,128)S(1)} %shard_map.48), channel_id=1, source_target_pairs={{0,128},{8,136},{16,144},{24,152},{32,160},{40,168},{48,176},{56,1... | collective-permute-start | bytes 98312 | tf_op jit(solution)/shard_map/ppermute | solution.py:170
  46.9 0.0 collective-permute-done.4.refs_2_
  46.9 1.3 %collective-permute-done.3.refs_1_ = f32[64,128]{1,0:T(8,128)S(1)} collective-permute-done((f32[64,128]{1,0:T(8,128)S(1)}, f32[64,128]{1,0:T(8,128)S(1)}, u32[]{:S(2)}, u32[]{:S(2)}) %collective-permute-start.3) | collective-permute-done | bytes 32800 | tf_op jit(solution)/shard_map/ppermute | solution.py:170
  48.2 0.3 collective-permute-done.2.refs_0_
  48.5 0.7 %shard_map.49 = bf16[16,64,128]{2,1,0:T(8,128)(2,1)} custom-call(bf16[16,64,128]{2,1,0:T(8,128)(2,1)S(1)} %all-to-all-done.slices_ref, f32[64,128]{1,0:T(8,128)S(1)} %collective-permute-done.2.refs_0_, f32[64,128]{1,0:T(8,128)S(1)} %collective-permute-done.3.refs_1_, f32[64,128]{1,0:T(8,128)S(1)} %collective-permute-done.4.refs_2_), custom_call_target="tpu_custom_call" | custom-call | flops 262144 | bytes 1048576 | tf_op jit(solution)/shard_map/pallas_call | solution.py:22
  49.2 5.1 %all-to-all-start.1 = ((bf16[16,64,128]{2,1,0:T(8,128)(2,1)}), bf16[16,64,128]{2,1,0:T(8,128)(2,1)S(1)}, u32[]{:S(2)}, u32[]{:S(2)}) async-start(bf16[16,64,128]{2,1,0:T(8,128)(2,1)} %shard_map.49), calls=%async_computation.1 | async-start | bytes 524288 | tf_op jit(solution)/shard_map/all_to_all | solution.py:177
  54.3 0.0 collective-permute-done.1.pair_hbm
  54.3 10.0 %all-to-all-done.1 = bf16[16,64,128]{2,1,0:T(8,128)(2,1)S(1)} async-done(((bf16[16,64,128]{2,1,0:T(8,128)(2,1)}), bf16[16,64,128]{2,1,0:T(8,128)(2,1)S(1)}, u32[]{:S(2)}, u32[]{:S(2)}) %all-to-all-start.1) | async-done | bytes 262176 | tf_op jit(solution)/shard_map/all_to_all | solution.py:177
  64.3 0.0 collective-permute-done.5.w_ref
  64.3 3.5 %shard_map.50 = bf16[368,1024]{1,0:T(8,128)(2,1)} custom-call(bf16[736,1024]{1,0:T(8,128)(2,1)} %collective-permute-done.1.pair_hbm, bf16[1024,128]{1,0:T(8,128)(2,1)S(1)} %bitcast.7, bf16[1024,1024]{1,0:T(8,128)(2,1)S(1)} %collective-permute-done.5.w_ref), custom_call_target="tpu_custom_call" | custom-call | flops 868220928 | bytes 6291456 | tf_op jit(solution)/shard_map/pallas_call | solution.py:22
  (1 shorter events, 0.0 us)
Async XLA Ops:
  2.5 6.1 %collective-permute-start = (bf16[1024,128]{1,0:T(8,128)(2,1)}, bf16[1024,128]{1,0:T(8,128)(2,1)}, u32[]{:S(2)}, u32[]{:S(2)}) collective-permute-start(bf16[1024,128]{1,0:T(8,128)(2,1)} %shard_map.46.after_ref), channel_id=1, source_target_pairs={{7,0},{0,1},{1,2},{2,3},{3,4},{4,5},{5,6},{6,7},{15,8},{8,9},{9,10... | collective-permute-start | bytes 786440 | tf_op jit(solution)/shard_map/ppermute | solution.py:140
  8.6 55.7 %collective-permute-start.5 = (bf16[1024,1024]{1,0:T(8,128)(2,1)}, bf16[1024,1024]{1,0:T(8,128)(2,1)S(1)}, u32[]{:S(2)}, u32[]{:S(2)}) collective-permute-start(bf16[1024,1024]{1,0:T(8,128)(2,1)} %bitcast.13), channel_id=1, source_target_pairs={{7,0},{0,1},{1,2},{2,3},{3,4},{4,5},{5,6},{6,7},{15,8},{8,9},{9,10... | collective-permute-start | bytes 6291464 | tf_op jit(solution)/shard_map/ppermute | solution.py:140
  13.0 15.3 %all-to-all-start = ((bf16[16,64,128]{2,1,0:T(8,128)(2,1)}), bf16[16,64,128]{2,1,0:T(8,128)(2,1)S(1)}, u32[]{:S(2)}, u32[]{:S(2)}) async-start(bf16[16,64,128]{2,1,0:T(8,128)(2,1)} %bitcast.4), calls=%async_computation | async-start | bytes 524288 | tf_op jit(solution)/shard_map/all_to_all | solution.py:163
  17.3 37.1 %collective-permute-start.1 = (bf16[736,1024]{1,0:T(8,128)(2,1)}, bf16[736,1024]{1,0:T(8,128)(2,1)}, u32[]{:S(2)}, u32[]{:S(2)}) collective-permute-start(bf16[736,1024]{1,0:T(8,128)(2,1)} %shard_map.47), channel_id=1, source_target_pairs={{7,0},{0,1},{1,2},{2,3},{3,4},{4,5},{5,6},{6,7},{15,8},{8,9},{9,10... | collective-permute-start | bytes 4521992 | tf_op jit(solution)/shard_map/ppermute | solution.py:140
  28.4 18.5 %collective-permute-start.4 = (f32[64,128]{1,0:T(8,128)S(1)}, f32[64,128]{1,0:T(8,128)S(1)}, u32[]{:S(2)}, u32[]{:S(2)}) collective-permute-start(f32[64,128]{1,0:T(8,128)S(1)} %shard_map.48), channel_id=1, source_target_pairs={{0,256},{8,264},{16,272},{24,280},{32,288},{40,296},{48,304},{56,3... | collective-permute-start | bytes 98312 | tf_op jit(solution)/shard_map/ppermute | solution.py:170
  41.9 6.3 %collective-permute-start.3 = (f32[64,128]{1,0:T(8,128)S(1)}, f32[64,128]{1,0:T(8,128)S(1)}, u32[]{:S(2)}, u32[]{:S(2)}) collective-permute-start(f32[64,128]{1,0:T(8,128)S(1)} %shard_map.48), channel_id=1, source_target_pairs={{0,384},{8,392},{16,400},{24,408},{32,416},{40,424},{48,432},{56,4... | collective-permute-start | bytes 98312 | tf_op jit(solution)/shard_map/ppermute | solution.py:170
  43.2 5.2 %collective-permute-start.2 = (f32[64,128]{1,0:T(8,128)S(1)}, f32[64,128]{1,0:T(8,128)S(1)}, u32[]{:S(2)}, u32[]{:S(2)}) collective-permute-start(f32[64,128]{1,0:T(8,128)S(1)} %shard_map.48), channel_id=1, source_target_pairs={{0,128},{8,136},{16,144},{24,152},{32,160},{40,168},{48,176},{56,1... | collective-permute-start | bytes 98312 | tf_op jit(solution)/shard_map/ppermute | solution.py:170
  49.2 15.1 %all-to-all-start.1 = ((bf16[16,64,128]{2,1,0:T(8,128)(2,1)}), bf16[16,64,128]{2,1,0:T(8,128)(2,1)S(1)}, u32[]{:S(2)}, u32[]{:S(2)}) async-start(bf16[16,64,128]{2,1,0:T(8,128)(2,1)} %shard_map.49), calls=%async_computation.1 | async-start | bytes 524288 | tf_op jit(solution)/shard_map/all_to_all | solution.py:177
